TPU v7x, 32 devices: a whole 2x2x4 slice. The times are simulated.
32 devices in a mesh: expert: 8 (over y, x, core), tensor: 4 (over z).
Axes of the slice: x: 2, y: 2, z: 4, core: 2. Of those that a mesh axis runs over, the one named last changes fastest.
Arguments:
- tokens: bfloat16 [4096, 1024], P('expert'), may hold values from -6 to 6
- norm1_gain: float32 [1024], replicated, may hold values from 0.5 to 1.5
- w_query: bfloat16 [1024, 1024], P(None, 'tensor'), may hold values from -0.1875 to 0.1875
- key_projection_weight: bfloat16 [1024, 512], P(None, 'tensor'), may hold values from -0.1875 to 0.1875
- value_projection_weight: bfloat16 [1024, 512], P(None, 'tensor'), may hold values from -0.1875 to 0.1875
- w_output: bfloat16 [1024, 1024], P('tensor'), may hold values from -1.5 to 1.5
- norm2_gain: float32 [1024], replicated, may hold values from 0.5 to 1.5
- w_router: bfloat16 [1024, 32], replicated, may hold values from -0.09375 to 0.09375
- expert_gate_weight: bfloat16 [32, 1024, 512], P('expert', None, 'tensor'), may hold values from -0.1875 to 0.1875
- expert_up_weight: bfloat16 [32, 1024, 512], P('expert', None, 'tensor'), may hold values from -0.1875 to 0.1875
- expert_down_weight: bfloat16 [32, 512, 1024], P('expert', 'tensor'), may hold values from -0.75 to 0.75
- expert_ids: int32 [4096, 8], P('expert'), may hold values from 0 to 31, all different within a row; in each aligned block of 512 rows (0 to 511, 512 to 1023, ...) at most 160 rows name the same one
- cotangent: bfloat16 [4096, 1024], P('expert'), may hold values from -6 to 6
Outputs:
- mixed: bfloat16 [4096, 1024], P('expert', 'tensor')
- grad_input: float32 [4096, 1024], P('expert')
- grad_norm1: float32 [1024], replicated
- grad_query: float32 [1024, 1024], P(None, 'tensor')
- grad_key: float32 [1024, 512], P(None, 'tensor')
- grad_value: float32 [1024, 512], P(None, 'tensor')
- grad_output: float32 [1024, 1024], P('tensor')
- grad_norm2: float32 [1024], replicated
- grad_router: float32 [1024, 32], replicated
- grad_gate: float32 [32, 1024, 512], P('expert', None, 'tensor')
- up_weight_gradient: float32 [32, 1024, 512], P('expert', None, 'tensor')
- grad_down: float32 [32, 512, 1024], P('expert', 'tensor')
Inputs may be any that keep to these rules, and one draw needn't show every extreme that they name: `expert_ids`: within the rows of one index of expert (512 tokens), no expert is named more than 160 times, a bound that some block reaches.
All inputs are finite; a program needn't handle non-finite values.
Results may differ from a plain program's by a relative error of at most 0.023.
Values may be sent and summed in bfloat16 or wider, within the bound.
No kernel may reach another device: no remote copies, remote signals or barrier semaphores. Data moves between devices by JAX's collectives and lax.ppermute only.
A program may use at most 192 MiB of HBM per device.

v0:
```python
import functools
import math

import jax
import jax.numpy as jnp
from jax import lax
from jax.experimental import pallas as pl
from jax.experimental.pallas import tpu as pltpu
from jax.sharding import PartitionSpec as P

HEAD_DIMENSION = 64
SEQ_LEN = 512

EPS = 1e-06
SCALE = 0.125
NEGATIVE = -1e30
THETA = 10000.0
F32 = jnp.float32
BF16 = jnp.bfloat16
EXACT = lax.Precision.HIGHEST
LANES = 128
TILE = 256


def tables(tok_count):
    half = HEAD_DIMENSION // 2
    freq = jnp.exp(-math.log(THETA) * jnp.arange(half, dtype=F32) / half)
    places = (jnp.arange(tok_count) % SEQ_LEN).astype(F32)
    angle = places[:, None] * freq[None, :]
    return (jnp.cos(angle)[:, None, :], jnp.sin(angle)[:, None, :])


def rotate(field, cosine, sine_table, factor):
    half = HEAD_DIMENSION // 2
    first = field[..., :half]
    second = field[..., half:]
    return jnp.concatenate(
        [
            first * cosine - factor * second * sine_table,
            second * cosine + factor * first * sine_table,
        ],
        axis=-1,
    )


def causal_mask():
    places = jnp.arange(SEQ_LEN)
    return places[:, None] >= places[None, :]


def attend_forward(query_rows, rotated_keys, value_rows):
    scores = (
        jnp.einsum("lkgd,mkd->kglm", query_rows, rotated_keys, preferred_element_type=F32) * SCALE
    )
    scores = jnp.where(causal_mask(), scores, NEGATIVE)
    highest = jnp.max(scores, axis=-1, keepdims=True)
    expanded = jnp.exp(scores - highest)
    summed = jnp.sum(expanded, axis=-1, keepdims=True)
    probability = (expanded / summed).astype(BF16)
    heads_out = jnp.einsum("kglm,mkd->lkgd", probability, value_rows, preferred_element_type=F32)
    return (heads_out.astype(BF16), (highest + jnp.log(summed))[..., 0])


def attend_backward(query_rows, rotated_keys, value_rows, grad_heads, log_total):
    scores = (
        jnp.einsum("lkgd,mkd->kglm", query_rows, rotated_keys, preferred_element_type=F32) * SCALE
    )
    probability = jnp.where(causal_mask(), jnp.exp(scores - log_total[..., None]), 0.0)
    prob_low = probability.astype(BF16)
    grad_values = jnp.einsum("kglm,lkgd->mkd", prob_low, grad_heads, preferred_element_type=F32)
    grad_prob = jnp.einsum("lkgd,mkd->kglm", grad_heads, value_rows, preferred_element_type=F32)
    row_delta = jnp.sum(probability * grad_prob, axis=-1, keepdims=True)
    grad_scores = (probability * (grad_prob - row_delta)).astype(BF16)
    grad_queries = (
        jnp.einsum("kglm,mkd->lkgd", grad_scores, rotated_keys, preferred_element_type=F32) * SCALE
    )
    grad_keys = (
        jnp.einsum("kglm,lkgd->mkd", grad_scores, query_rows, preferred_element_type=F32) * SCALE
    )
    return (grad_queries, grad_keys, grad_values)


def mm(left, right):
    return jnp.dot(left, right, preferred_element_type=F32)


def mm_rows(left, right):
    return lax.dot_general(left, right, (((0,), (0,)), ((), ())), preferred_element_type=F32)


def mm_cols(left, right):
    return lax.dot_general(left, right, (((1,), (1,)), ((), ())), preferred_element_type=F32)


def piece(array, index, size, axis=0):
    return lax.dynamic_slice_in_dim(array, index * size, size, axis)


def swap(array, mask):
    size = lax.axis_size("expert")
    return lax.ppermute(array, "expert", [(i, i ^ mask) for i in range(size)])


def z_shift(array, step):
    size = lax.axis_size("tensor")
    return lax.ppermute(array, "tensor", [(i, (i + step) % size) for i in range(size)])


def z_received(array):
    return [array] + [z_shift(array, step) for step in range(1, lax.axis_size("tensor"))]


def z_place(parts):
    size, mine = lax.axis_size("tensor"), lax.axis_index("tensor")
    rows = parts[0].shape[0]
    whole = jnp.zeros((rows * size,) + parts[0].shape[1:], parts[0].dtype)
    for step, part in enumerate(parts):
        whole = lax.dynamic_update_slice_in_dim(whole, part, (mine + size - step) % size * rows, 0)
    return whole


def z_scatter(array, axis=0):
    size, mine = lax.axis_size("tensor"), lax.axis_index("tensor")
    width = array.shape[axis] // size
    total = piece(array, mine, width, axis).astype(F32)
    for step in range(1, size):
        sent = piece(array, (mine + step) % size, width, axis).astype(BF16)
        total = total + z_shift(sent, step).astype(F32)
    return total


def same_core_groups():
    size = lax.axis_size("expert")
    return [list(range(0, size, 2)), list(range(1, size, 2))]


def plane_gather(array):
    if lax.axis_size("expert") != 8:
        return [
            lax.all_gather(
                array, "expert", axis=0, tiled=True, axis_index_groups=same_core_groups()
            )
        ]
    half = array.shape[0] // 2
    from_x = swap(array, 2)
    from_y = swap(array, 4)
    return [array, from_x, from_y, swap(from_x[:half], 4), swap(from_y[half:], 2)]


def plane_scatter(blocks):
    if lax.axis_size("expert") != 8:
        return lax.psum_scatter(
            blocks[0].astype(BF16),
            "expert",
            scatter_dimension=0,
            tiled=True,
            axis_index_groups=same_core_groups(),
        ).astype(F32)
    own, for_x, for_y, far_x, far_y = blocks
    half = own.shape[0] // 2
    via_x = swap(far_x, 2).astype(F32)
    via_y = swap(far_y, 4).astype(F32)
    for_y = for_y.at[:half].set((for_y[:half].astype(F32) + via_x).astype(BF16))
    for_x = for_x.at[half:].set((for_x[half:].astype(F32) + via_y).astype(BF16))
    return own.astype(F32) + swap(for_x, 2).astype(F32) + swap(for_y, 4).astype(F32)


def expert_sum(array):
    if lax.axis_size("expert") != 8:
        return lax.psum(array.astype(BF16), "expert").astype(F32)
    place = lax.axis_index("expert")
    core, chip = place % 2, place // 2
    half = array.shape[0] // 2
    rows = half // 4
    array = array.astype(BF16)
    mine = piece(array, core, half).astype(F32)
    mine = mine + swap(piece(array, 1 - core, half), 1).astype(F32)
    total = piece(mine, chip, rows)
    for mask in (1, 2, 3):
        total = total + swap(piece(mine, chip ^ mask, rows).astype(BF16), 2 * mask).astype(F32)
    total = total.astype(BF16)
    gathered = jnp.zeros((half,) + array.shape[1:], BF16)
    for mask in (0, 1, 2, 3):
        part = swap(total, 2 * mask) if mask else total
        gathered = lax.dynamic_update_slice_in_dim(gathered, part, (chip ^ mask) * rows, 0)
    both = jnp.concatenate([gathered, gathered])
    both = lax.dynamic_update_slice_in_dim(both, swap(gathered, 1), (1 - core) * half, 0)
    return both.astype(F32)


def expert_kernel(
    experts,
    top_count,
    units,
    names_ref,
    normed_ref,
    grad_ref,
    router_ref,
    gate_ref,
    up_ref,
    down_ref,
    out_ref,
    rows_ref,
    gate_grad_ref,
    up_grad_ref,
    inner_ref,
):
    tile, model_width = normed_ref.shape
    width = gate_ref.shape[1]
    normed = normed_ref[...]
    grad = grad_ref[:, :model_width]
    chosen_names = grad_ref[:, model_width:].astype(F32)
    lane = lax.broadcasted_iota(jnp.int32, (tile, LANES), 1)
    lane_float = lane.astype(F32)
    chosen = lane_float == chosen_names[:, 0:1]
    for k in range(1, top_count):
        chosen = chosen | (lane_float == chosen_names[:, k : k + 1])
    logits = jnp.where(chosen, mm(normed, router_ref[...]), NEGATIVE)
    expanded = jnp.exp(logits - jnp.max(logits, axis=-1, keepdims=True))
    expanded = jnp.where(chosen, expanded, 0.0)
    routing = expanded / jnp.sum(expanded, axis=-1, keepdims=True)
    grad_routing = jnp.zeros((tile, LANES), F32)
    columns = min(TILE, width)
    for start in range(0, width, columns):
        part = slice(start, start + columns)
        gate_act = mm(normed, gate_ref[:, part])
        up_act = mm(normed, up_ref[:, part])
        grad_plain = mm_cols(grad, down_ref[part, :])
        weights = []
        for e in range(start // units, (start + columns) // units):
            weight = jnp.sum(
                jnp.where(lane == names_ref[e], routing, 0.0), axis=-1, keepdims=True
            )
            weights.append(jnp.broadcast_to(weight, (tile, units)))
        wide = jnp.concatenate(weights, axis=1) if len(weights) > 1 else weights[0]
        sigmoid_gate = jax.nn.sigmoid(gate_act)
        swish = gate_act * sigmoid_gate
        inner = swish * up_act
        inner_grad = inner * grad_plain
        for i, e in enumerate(range(start // units, (start + columns) // units)):
            total = jnp.sum(inner_grad[:, i * units : (i + 1) * units], axis=-1, keepdims=True)
            grad_routing = jnp.where(lane == names_ref[e], total, grad_routing)
        grad_inner = grad_plain * wide
        inner_ref[:, part] = (inner * wide).astype(BF16)
        up_grad_ref[:, part] = (grad_inner * swish).astype(BF16)
        gate_grad_ref[:, part] = (
            grad_inner * up_act * (sigmoid_gate + swish * (1.0 - sigmoid_gate))
        ).astype(BF16)
    rounded = grad_routing.astype(BF16).astype(F32)
    left = pltpu.roll(grad_routing - rounded, experts, 1)
    rows_ref[:, model_width:] = (rounded + left).astype(BF16)
    rows_ref[:, :model_width] = (
        mm_cols(gate_grad_ref[...], gate_ref[...]) + mm_cols(up_grad_ref[...], up_ref[...])
    ).astype(BF16)
    out_ref[...] = mm(inner_ref[...], down_ref[...]).astype(BF16)


def expert_block(names, normed, grad, router, gate_w, up_w, down_w, experts, top_count, units):
    rows, model_width = normed.shape
    width = gate_w.shape[1]
    tile = min(TILE, rows)

    def tiled(columns):
        return pl.BlockSpec((tile, columns), lambda i, names: (i, 0))

    def fixed(array):
        return pl.BlockSpec(array.shape, lambda i, names: (0, 0))

    def shaped(columns):
        return jax.ShapeDtypeStruct((rows, columns), BF16)

    return pl.pallas_call(
        functools.partial(expert_kernel, experts, top_count, units),
        grid_spec=pltpu.PrefetchScalarGridSpec(
            num_scalar_prefetch=1,
            grid=(rows // tile,),
            in_specs=[
                tiled(model_width),
                tiled(model_width + LANES),
                fixed(router),
                fixed(gate_w),
                fixed(up_w),
                fixed(down_w),
            ],
            out_specs=[
                tiled(model_width),
                tiled(model_width + LANES),
                tiled(width),
                tiled(width),
                tiled(width),
            ],
        ),
        out_shape=[
            shaped(model_width),
            shaped(model_width + LANES),
            shaped(width),
            shaped(width),
            shaped(width),
        ],
        compiler_params=pltpu.CompilerParams(vmem_limit_bytes=44 * 1024 * 1024),
        cost_estimate=pl.CostEstimate(
            flops=12 * rows * model_width * width,
            bytes_accessed=6 * model_width * width + 14 * rows * model_width,
            transcendentals=rows * width,
        ),
        name="experts",
    )(names, normed, grad, router, gate_w, up_w, down_w)


def tied(*arrays):
    return lax.optimization_barrier(arrays)


def norm_scale(field):
    return lax.rsqrt(jnp.mean(field * field, axis=-1, keepdims=True) + EPS)


def route(normed, router, chosen):
    logits = mm(normed, router)
    masked = jnp.where(chosen, logits, NEGATIVE)
    highest = jnp.max(masked, axis=-1, keepdims=True)
    expanded = jnp.where(chosen, jnp.exp(masked - highest), 0.0)
    return expanded / jnp.sum(expanded, axis=-1, keepdims=True)


def local(
    tokens,
    norm1_gain,
    w_query,
    key_projection_weight,
    value_projection_weight,
    w_output,
    norm2_gain,
    w_router,
    expert_gate_weight,
    expert_up_weight,
    expert_down_weight,
    expert_ids,
    cotangent,
):
    tok_count = tokens.shape[0]
    model_width = tokens.shape[1]
    experts, top_count = w_router.shape[1], expert_ids.shape[1]
    here, units = expert_gate_weight.shape[0], expert_gate_weight.shape[2]
    heads_query = w_query.shape[1] // HEAD_DIMENSION
    heads_kv = key_projection_weight.shape[1] // HEAD_DIMENSION
    group_size = heads_query // heads_kv
    cosine, sine_table = tables(tok_count)
    expert_count = lax.axis_size("expert")
    tensor_count = lax.axis_size("tensor")
    expert_place = lax.axis_index("expert")
    tensor_place = lax.axis_index("tensor")
    core = expert_place % 2
    own_rows = tok_count // tensor_count
    col_width = model_width // tensor_count

    names_wide = jnp.pad(expert_ids.astype(BF16), ((0, 0), (0, LANES - top_count)))
    grad_blocks = plane_gather(jnp.concatenate([cotangent, names_wide], axis=1))
    if expert_count == 8:
        grad_blocks, grad_far = grad_blocks[:3], grad_blocks[3:]

    half = w_output.shape[0] // 2
    w_halves = [z_shift(piece(w_output, core, half), step) for step in range(1, tensor_count)]
    expert_weights = [expert_gate_weight, expert_up_weight, expert_down_weight]
    if expert_count == 8:
        grad_blocks, w_halves = tied(grad_blocks, w_halves)
    w_halves = jnp.stack(w_halves)
    w_others = swap(w_halves, 1)
    w_parts = jnp.where(
        core == 0,
        jnp.concatenate([w_halves, w_others], axis=1),
        jnp.concatenate([w_others, w_halves], axis=1),
    )

    resid_in = tokens.astype(F32)
    first_scale = norm_scale(resid_in)
    first_norm = (resid_in * first_scale * norm1_gain).astype(BF16)
    query_raw = mm(first_norm, w_query).reshape(tok_count, heads_query, HEAD_DIMENSION)
    key_raw = mm(first_norm, key_projection_weight).reshape(tok_count, heads_kv, HEAD_DIMENSION)
    query_rows = (
        rotate(query_raw, cosine, sine_table, 1.0)
        .astype(BF16)
        .reshape(tok_count, heads_kv, group_size, HEAD_DIMENSION)
    )
    rotated_keys = rotate(key_raw, cosine, sine_table, 1.0).astype(BF16)
    value_rows = (
        mm(first_norm, value_projection_weight)
        .astype(BF16)
        .reshape(tok_count, heads_kv, HEAD_DIMENSION)
    )
    attended, log_total = attend_forward(query_rows, rotated_keys, value_rows)
    attended = attended.reshape(tok_count, heads_query * HEAD_DIMENSION)

    attended_parts = z_received(attended)

    resid_in, attended_parts, expert_weights, w_parts = tied(
        resid_in, attended_parts, expert_weights, w_parts
    )
    other_weights = [swap(weight, 1) for weight in expert_weights]
    attended = attended_parts[0]

    def as_columns(weight):
        return weight.transpose(1, 0, 2).reshape(model_width, -1)

    chip_weights = [jnp.concatenate(pair) for pair in zip(expert_weights, other_weights)]
    gate_w, up_w = as_columns(chip_weights[0]), as_columns(chip_weights[1])
    down_w = chip_weights[2].reshape(-1, model_width)
    hidden = resid_in + mm(attended, w_output)
    for step in range(1, tensor_count):
        hidden = hidden + mm(attended_parts[step], w_parts[step - 1])
    second_scale = norm_scale(hidden)
    second_norm = (hidden * second_scale * norm2_gain).astype(BF16)

    local_names = jnp.concatenate(
        [
            expert_place * here + jnp.arange(here, dtype=jnp.int32),
            (expert_place ^ 1) * here + jnp.arange(here, dtype=jnp.int32),
        ]
    )
    router_wide = jnp.pad(w_router, ((0, 0), (0, LANES - experts)))
    if expert_count == 8:
        second_norm, grad_far = tied(second_norm, grad_far)
        grad_blocks = grad_blocks + grad_far
    normed_blocks = plane_gather(second_norm)
    done = [
        expert_block(
            local_names,
            normed,
            grad,
            router_wide,
            gate_w,
            up_w,
            down_w,
            experts,
            top_count,
            units,
        )
        for normed, grad in zip(normed_blocks, grad_blocks)
    ]
    plane_rows = plane_scatter([block[1] for block in done])
    plane_rows, *out_blocks = tied(plane_rows, *[block[0] for block in done])
    held = tied(*[array for block in done for array in block[2:]])
    done = [held[3 * i : 3 * i + 3] for i in range(len(done))]
    gate_total = up_total = down_total = 0.0
    for normed, grad, block in zip(normed_blocks, grad_blocks, done):
        gate_total = gate_total + mm_rows(normed, block[0])
        up_total = up_total + mm_rows(normed, block[1])
        down_total = down_total + mm_rows(block[2], grad[:, :model_width])

    row_sum = z_scatter(plane_rows)
    plane_out = plane_scatter(out_blocks)
    row_sum, gate_total, up_total, down_total = tied(row_sum, gate_total, up_total, down_total)

    width = here * units

    def from_chip(total):
        return total[:, :width] + swap(total[:, width:].astype(BF16), 1).astype(F32)

    def as_experts(total):
        return total.reshape(model_width, here, units).transpose(1, 0, 2)

    grad_gate = as_experts(from_chip(gate_total))
    up_weight_gradient = as_experts(from_chip(up_total))
    grad_down = down_total[:width] + swap(down_total[width:].astype(BF16), 1).astype(F32)
    grad_down = grad_down.reshape(here, units, model_width)
    my_routing_grad = (
        row_sum[:, model_width : model_width + experts]
        + row_sum[:, model_width + experts : model_width + 2 * experts]
    )
    row_sum = row_sum[:, :model_width]

    def mine(array):
        return piece(array, tensor_place, own_rows)

    my_hidden, my_scale = mine(hidden), mine(second_scale)
    my_normed = mine(second_norm)
    names = jnp.arange(experts, dtype=jnp.int32)
    my_chosen = jnp.any(mine(expert_ids)[:, :, None] == names[None, None, :], axis=1)
    my_routing = route(my_normed, w_router, my_chosen)
    my_normed = my_normed.astype(F32)
    my_logits = my_routing * (
        my_routing_grad - jnp.sum(my_routing * my_routing_grad, axis=-1, keepdims=True)
    )
    router_float = w_router.astype(F32)
    grad_second = row_sum + jnp.dot(my_logits, router_float.T, precision=EXACT)
    grad_router = lax.dot_general(
        my_logits, my_normed, (((0,), (0,)), ((), ())), precision=EXACT
    )
    grad_norm2 = jnp.sum(grad_second * my_hidden * my_scale, axis=0)
    gained_two = grad_second * norm2_gain
    my_grad_hidden = (
        mine(cotangent).astype(F32)
        + my_scale * gained_two
        - my_hidden * my_scale**3 * jnp.mean(gained_two * my_hidden, axis=-1, keepdims=True)
    )
    small = jnp.concatenate([grad_router, grad_norm2[None]])
    extra = -small.shape[0] % 16
    small = jnp.pad(small, ((0, extra), (0, 0))).astype(BF16)
    parts = z_received(jnp.concatenate([my_grad_hidden.astype(BF16), small]))
    grad_gate, up_weight_gradient, grad_down, *parts = tied(
        grad_gate, up_weight_gradient, grad_down, *parts
    )
    routed = z_scatter(plane_out, axis=1)
    mixed = (piece(hidden, tensor_place, col_width, 1) + routed).astype(BF16)
    grad_branch = z_place([part[:own_rows] for part in parts])
    small = sum(part[own_rows:].astype(F32) for part in parts)
    grad_output = mm_rows(attended, grad_branch)

    grad_heads = mm_cols(grad_branch, w_output).astype(BF16)
    grad_heads = grad_heads.reshape(tok_count, heads_kv, group_size, HEAD_DIMENSION)
    grad_queries, grad_keys, grad_values = attend_backward(
        query_rows, rotated_keys, value_rows, grad_heads, log_total
    )
    grad_query_raw = rotate(
        grad_queries.reshape(tok_count, heads_query, HEAD_DIMENSION), cosine, sine_table, -1.0
    )
    grad_query_raw = grad_query_raw.reshape(tok_count, -1).astype(BF16)
    grad_key_raw = rotate(grad_keys, cosine, sine_table, -1.0)
    grad_key_raw = grad_key_raw.reshape(tok_count, -1).astype(BF16)
    grad_value_raw = grad_values.reshape(tok_count, -1).astype(BF16)
    grad_raw = jnp.concatenate([grad_query_raw, grad_key_raw, grad_value_raw], axis=1)
    grad_first = (
        mm_cols(grad_query_raw, w_query)
        + mm_cols(grad_key_raw, key_projection_weight)
        + mm_cols(grad_value_raw, value_projection_weight)
    )
    norm1_part = sum(z_received(jnp.sum(grad_first * resid_in * first_scale, axis=0)[None]))

    grad_raw = mm_rows(first_norm, grad_raw)
    raw_width = grad_raw.shape[1]

    def folded(array):
        array = jnp.pad(array.astype(BF16), ((0, -array.shape[0] % 16), (0, 0)))
        return [array[:, i : i + raw_width] for i in range(0, model_width, raw_width)]

    pile = [grad_raw.astype(BF16)] + folded(grad_output) + folded(small) + folded(norm1_part)
    places = [0]
    for part in pile:
        places.append(places[-1] + part.shape[0])
    extra = -places[-1] % 128
    pile = expert_sum(jnp.concatenate(pile + [jnp.zeros((extra, raw_width), BF16)]))
    grad_weights = pile[: places[1]]
    folds = model_width // raw_width

    def unfolded(first, rows):
        return jnp.concatenate(
            [pile[places[i] : places[i] + rows] for i in range(first, first + folds)], axis=1
        )

    grad_output = unfolded(1, grad_output.shape[0])
    small = unfolded(1 + folds, experts + 1)
    grad_norm1 = unfolded(1 + 2 * folds, 1)[0]
    q_width, k_width = w_query.shape[1], key_projection_weight.shape[1]

    mixed, grad_first = tied(mixed, grad_first)
    grad_first = z_scatter(grad_first)
    gained_one = grad_first * norm1_gain
    my_resid, my_first_scale = mine(resid_in), mine(first_scale)
    my_grad_input = (
        my_grad_hidden
        + my_first_scale * gained_one
        - my_resid * my_first_scale**3 * jnp.mean(gained_one * my_resid, axis=-1, keepdims=True)
    )
    grad_input = z_place(z_received(my_grad_input.astype(BF16))).astype(F32)

    return (
        mixed,
        grad_input,
        grad_norm1,
        grad_weights[:, :q_width],
        grad_weights[:, q_width : q_width + k_width],
        grad_weights[:, q_width + k_width :],
        grad_output,
        small[experts],
        small[:experts].T,
        grad_gate,
        up_weight_gradient,
        grad_down,
    )


def solution(mesh):
    placed = (
        P("expert", None),
        P(),
        P(None, "tensor"),
        P(None, "tensor"),
        P(None, "tensor"),
        P("tensor", None),
        P(),
        P(),
        P("expert", None, "tensor"),
        P("expert", None, "tensor"),
        P("expert", "tensor", None),
        P("expert", None),
        P("expert", None),
    )
    return jax.shard_map(
        local,
        mesh=mesh,
        in_specs=placed,
        out_specs=(
            P("expert", "tensor"),
            P("expert", None),
            P(),
            P(None, "tensor"),
            P(None, "tensor"),
            P(None, "tensor"),
            P("tensor", None),
            P(),
            P(),
            P("expert", None, "tensor"),
            P("expert", None, "tensor"),
            P("expert", "tensor", None),
        ),
        check_vma=False,
    )
```

profile of v0, /device:TPU:9, one launch (start us, length us, event | category | flops | bytes accessed | tf_op | source)
XLA Modules:
  0.0 430.3 jit_solution(12486831034898125545)
XLA Ops:
  16.7 11.4 %collective-permute-done.6 = bf16[128,1024]{1,0:T(8,128)(2,1)S(1)} collective-permute-done((bf16[128,1024]{1,0:T(8,128)(2,1)S(1)}, bf16[128,1024]{1,0:T(8,128)(2,1)S(1)}, u32[]{:S(2)}, u32[]{:S(2)}) %collective-permute-start.6) | collective-permute-done | bytes 262176 | tf_op jit(solution)/shard_map/ppermute | solution.py:106
  46.0 13.7 %collective-permute-done.1 = bf16[512,256]{0,1:T(8,128)(2,1)} collective-permute-done((bf16[512,256]{0,1:T(8,128)(2,1)S(1)}, bf16[512,256]{0,1:T(8,128)(2,1)}, u32[]{:S(2)}, u32[]{:S(2)}) %collective-permute-start.1) | collective-permute-done | bytes 262176 | tf_op jit(solution)/shard_map/ppermute | solution.py:106
  79.7 15.3 %collective-permute-done.14.normed_ref = bf16[512,1024]{1,0:T(8,128)(2,1)} collective-permute-done((bf16[512,1024]{1,0:T(8,128)(2,1)S(1)}, bf16[512,1024]{1,0:T(8,128)(2,1)}, u32[]{:S(2)}, u32[]{:S(2)}) %collective-permute-start.14) | collective-permute-done | bytes 1048608 | tf_op jit(solution)/shard_map/ppermute | solution.py:101
  105.9 10.4 %experts.5 = (bf16[512,1024]{1,0:T(8,128)(2,1)S(1)}, bf16[512,1152]{1,0:T(8,128)(2,1)S(1)}, bf16[512,1024]{1,0:T(8,128)(2,1)S(1)}, bf16[512,1024]{1,0:T(8,128)(2,1)S(1)}, bf16[512,1024]{1,0:T(8,128)(2,1)S(1)}) custom-call(s32[8]{0:T(128)S(1)} %pad_add_fusion.names_ref, bf16[512,1024]{1,0:T(8,128)(2,1)S(1)} %multiply_convert_fusion.normed_ref, ...), custom_call_target="tpu_custom_call" | custom-call | flops 6442450944 | bytes 13631488 | tf_op jit(solution)/shard_map/experts/pallas_call | solution.py:272
  120.3 10.6 %experts.8 = (bf16[512,1024]{1,0:T(8,128)(2,1)S(1)}, bf16[512,1152]{1,0:T(8,128)(2,1)S(1)}, bf16[512,1024]{1,0:T(8,128)(2,1)S(1)}, bf16[512,1024]{1,0:T(8,128)(2,1)S(1)}, bf16[512,1024]{1,0:T(8,128)(2,1)S(1)}) custom-call(s32[8]{0:T(128)S(1)} %pad_add_fusion.names_ref, bf16[512,1024]{1,0:T(8,128)(2,1)S(1)} %collective-permute-done.15.normed_ref, ...), custom_call_target="tpu_custom_call" | custom-call | flops 6442450944 | bytes 13631488 | tf_op jit(solution)/shard_map/experts/pallas_call | solution.py:272
  136.0 11.2 %experts.6 = (bf16[512,1024]{1,0:T(8,128)(2,1)S(1)}, bf16[512,1152]{1,0:T(8,128)(2,1)S(1)}, bf16[512,1024]{1,0:T(8,128)(2,1)S(1)}, bf16[512,1024]{1,0:T(8,128)(2,1)S(1)}, bf16[512,1024]{1,0:T(8,128)(2,1)S(1)}) custom-call(s32[8]{0:T(128)S(1)} %pad_add_fusion.names_ref, bf16[512,1024]{1,0:T(8,128)(2,1)} %collective-permute-done.14.normed_ref, ...), custom_call_target="tpu_custom_call" | custom-call | flops 6442450944 | bytes 13631488 | tf_op jit(solution)/shard_map/experts/pallas_call | solution.py:272
  153.8 4.9 %experts.9 = (bf16[256,1024]{1,0:T(8,128)(2,1)S(1)}, bf16[256,1152]{1,0:T(8,128)(2,1)}, bf16[256,1024]{1,0:T(8,128)(2,1)S(1)}, bf16[256,1024]{1,0:T(8,128)(2,1)S(1)}, bf16[256,1024]{1,0:T(8,128)(2,1)S(1)}) custom-call(s32[8]{0:T(128)S(1)} %pad_add_fusion.names_ref, bf16[256,1024]{1,0:T(8,128)(2,1)S(1)} %collective-permute-done.19.normed_ref, ...), custom_call_target="tpu_custom_call" | custom-call | flops 3221225472 | bytes 9961472 | tf_op jit(solution)/shard_map/experts/pallas_call | solution.py:272
  160.7 4.9 %experts.7 = (bf16[256,1024]{1,0:T(8,128)(2,1)S(1)}, bf16[256,1152]{1,0:T(8,128)(2,1)}, bf16[256,1024]{1,0:T(8,128)(2,1)S(1)}, bf16[256,1024]{1,0:T(8,128)(2,1)S(1)}, bf16[256,1024]{1,0:T(8,128)(2,1)S(1)}) custom-call(s32[8]{0:T(128)S(1)} %pad_add_fusion.names_ref, bf16[256,1024]{1,0:T(8,128)(2,1)S(1)} %collective-permute-done.16.normed_ref, ...), custom_call_target="tpu_custom_call" | custom-call | flops 3221225472 | bytes 9961472 | tf_op jit(solution)/shard_map/experts/pallas_call | solution.py:272
  178.0 5.6 %add_add_fusion = f32[1024,1024]{1,0:T(8,128)} fusion(f32[1024,1024]{1,0:T(8,128)S(1)} %fusion.48, f32[1024,1024]{1,0:T(8,128)S(1)} %fusion.24, f32[1024,1024]{1,0:T(8,128)S(1)} %fusion.28, f32[1024,1024]{1,0:T(8,128)} %fusion.26, bf16[256,1024]{1,0:T(8,128)(2,1)S(1)} %get-tuple-element.200, bf16[256,1152]{1,0:T(8,128)(2,1)S(1)} %collective-permute-done.10.grad_ref), kind=kOutput, calls=%fused_computation.9 | convolution fusion | flops 541065216 | bytes 22020096 | tf_op jit(solution)/shard_map/dot_general | solution.py:88
  186.9 4.7 %fusion.91 = f32[1024,1024]{1,0:T(8,128)} fusion(bf16[512,1024]{1,0:T(8,128)(2,1)} %collective-permute-done.14.normed_ref, bf16[512,1024]{1,0:T(8,128)(2,1)S(1)} %copy-done.22), kind=kOutput, calls=%fused_computation.218 | convolution fusion | flops 1073741824 | bytes 6291456 | tf_op jit(solution)/shard_map/dot_general | solution.py:88
  202.4 6.9 %add_add_fusion.2 = f32[1024,1024]{1,0:T(8,128)} fusion(f32[1024,1024]{1,0:T(8,128)S(1)} %fusion.93, f32[1024,1024]{1,0:T(8,128)} %fusion.92, f32[1024,1024]{1,0:T(8,128)S(1)} %fusion.90, f32[1024,1024]{1,0:T(8,128)} %fusion.91, bf16[256,1024]{1,0:T(8,128)(2,1)S(1)} %collective-permute-done.16.normed_ref, bf16[256,1024]{1,0:T(8,128)(2,1)S(1)} %get-tuple-element.190), kind=kOutput, calls=%fused_computation.11 | convolution fusion | flops 541065216 | bytes 22020096 | tf_op jit(solution)/shard_map/dot_general | solution.py:88
  209.2 14.4 %collective-permute-done.21 = bf16[512,1152]{1,0:T(8,128)(2,1)S(1)} collective-permute-done((bf16[512,1152]{1,0:T(8,128)(2,1)S(1)}, bf16[512,1152]{1,0:T(8,128)(2,1)S(1)}, u32[]{:S(2)}, u32[]{:S(2)}) %collective-permute-start.21) | collective-permute-done | bytes 1179680 | tf_op jit(solution)/shard_map/ppermute | solution.py:101
  237.2 9.7 %collective-permute-done.30 = bf16[128,1152]{1,0:T(8,128)(2,1)S(1)} collective-permute-done((bf16[128,1152]{1,0:T(8,128)(2,1)S(1)}, bf16[128,1152]{1,0:T(8,128)(2,1)S(1)}, u32[]{:S(2)}, u32[]{:S(2)}) %collective-permute-start.30) | collective-permute-done | bytes 294944 | tf_op jit(solution)/shard_map/ppermute | solution.py:106
  246.9 6.3 %collective-permute-done.29 = bf16[128,1152]{1,0:T(8,128)(2,1)S(1)} collective-permute-done((bf16[128,1152]{1,0:T(8,128)(2,1)S(1)}, bf16[128,1152]{1,0:T(8,128)(2,1)S(1)}, u32[]{:S(2)}, u32[]{:S(2)}) %collective-permute-start.29) | collective-permute-done | bytes 294944 | tf_op jit(solution)/shard_map/ppermute | solution.py:106
  273.6 20.9 %collective-permute-done.36 = bf16[176,1024]{1,0:T(8,128)(2,1)S(1)} collective-permute-done((bf16[176,1024]{1,0:T(8,128)(2,1)S(1)}, bf16[176,1024]{1,0:T(8,128)(2,1)S(1)}, u32[]{:S(2)}, u32[]{:S(2)}) %collective-permute-start.36) | collective-permute-done | bytes 360480 | tf_op jit(solution)/shard_map/ppermute | solution.py:106
  327.5 10.7 %collective-permute-done.27 = bf16[512,256]{1,0:T(8,128)(2,1)} collective-permute-done((bf16[512,256]{1,0:T(8,128)(2,1)}, bf16[512,256]{1,0:T(8,128)(2,1)}, u32[]{:S(2)}, u32[]{:S(2)}) %collective-permute-start.27) | collective-permute-done | bytes 262176 | tf_op jit(solution)/shard_map/ppermute | solution.py:106
  338.2 5.5 %collective-permute-done.26 = bf16[512,256]{1,0:T(8,128)(2,1)} collective-permute-done((bf16[512,256]{1,0:T(8,128)(2,1)S(1)}, bf16[512,256]{1,0:T(8,128)(2,1)}, u32[]{:S(2)}, u32[]{:S(2)}) %collective-permute-start.26) | collective-permute-done | bytes 262176 | tf_op jit(solution)/shard_map/ppermute | solution.py:106
  351.9 5.2 %collective-permute-done.40 = bf16[128,1024]{1,0:T(8,128)(2,1)S(1)} collective-permute-done((bf16[128,1024]{1,0:T(8,128)(2,1)}, bf16[128,1024]{1,0:T(8,128)(2,1)S(1)}, u32[]{:S(2)}, u32[]{:S(2)}) %collective-permute-start.40) | collective-permute-done | bytes 262176 | tf_op jit(solution)/shard_map/ppermute | solution.py:106
  357.0 7.3 %collective-permute-done.39 = bf16[128,1024]{1,0:T(8,128)(2,1)} collective-permute-done((bf16[128,1024]{1,0:T(8,128)(2,1)}, bf16[128,1024]{1,0:T(8,128)(2,1)}, u32[]{:S(2)}, u32[]{:S(2)}) %collective-permute-start.39) | collective-permute-done | bytes 262176 | tf_op jit(solution)/shard_map/ppermute | solution.py:106
  364.4 5.6 %collective-permute-done.38 = bf16[128,1024]{1,0:T(8,128)(2,1)} collective-permute-done((bf16[128,1024]{1,0:T(8,128)(2,1)}, bf16[128,1024]{1,0:T(8,128)(2,1)}, u32[]{:S(2)}, u32[]{:S(2)}) %collective-permute-start.38) | collective-permute-done | bytes 262176 | tf_op jit(solution)/shard_map/ppermute | solution.py:106
  375.7 4.6 %collective-permute-done.50 = bf16[208,512]{1,0:T(8,128)(2,1)S(1)} collective-permute-done((bf16[208,512]{1,0:T(8,128)(2,1)S(1)}, bf16[208,512]{1,0:T(8,128)(2,1)S(1)}, u32[]{:S(2)}, u32[]{:S(2)}) %collective-permute-start.50) | collective-permute-done | bytes 213024 | tf_op jit(solution)/shard_map/ppermute | solution.py:101
  380.3 5.4 %collective-permute-done.49 = bf16[208,512]{1,0:T(8,128)(2,1)S(1)} collective-permute-done((bf16[208,512]{1,0:T(8,128)(2,1)S(1)}, bf16[208,512]{1,0:T(8,128)(2,1)S(1)}, u32[]{:S(2)}, u32[]{:S(2)}) %collective-permute-start.49) | collective-permute-done | bytes 213024 | tf_op jit(solution)/shard_map/ppermute | solution.py:101
  393.6 5.2 %collective-permute-done.53 = bf16[208,512]{1,0:T(8,128)(2,1)S(1)} collective-permute-done((bf16[208,512]{1,0:T(8,128)(2,1)S(1)}, bf16[208,512]{1,0:T(8,128)(2,1)S(1)}, u32[]{:S(2)}, u32[]{:S(2)}) %collective-permute-start.53) | collective-permute-done | bytes 213024 | tf_op jit(solution)/shard_map/ppermute | solution.py:101
  405.1 15.8 %collective-permute-done.42 = bf16[128,1024]{1,0:T(8,128)(2,1)S(1)} collective-permute-done((bf16[128,1024]{1,0:T(8,128)(2,1)S(1)}, bf16[128,1024]{1,0:T(8,128)(2,1)S(1)}, u32[]{:S(2)}, u32[]{:S(2)}) %collective-permute-start.42) | collective-permute-done | bytes 262176 | tf_op jit(solution)/shard_map/ppermute | solution.py:106
  (419 shorter events, 211.7 us)
Async XLA Ops:
  3.0 28.7 %collective-permute-start.3 = (bf16[512,1152]{1,0:T(8,128)(2,1)S(1)}, bf16[512,1152]{1,0:T(8,128)(2,1)S(1)}, u32[]{:S(2)}, u32[]{:S(2)}) collective-permute-start(bf16[512,1152]{1,0:T(8,128)(2,1)S(1)} %fusion.15.grad_ref), channel_id=1, source_target_pairs={{0,8},{4,12},{8,0},{12,4},{16,24},{20,28},{24,16},{28,20},{1,9},{5... | collective-permute-start | bytes 3538952 | tf_op jit(solution)/shard_map/ppermute | solution.py:101
  4.2 27.4 %collective-permute-start.4 = (bf16[512,1152]{1,0:T(8,128)(2,1)S(1)}, bf16[512,1152]{1,0:T(8,128)(2,1)}, u32[]{:S(2)}, u32[]{:S(2)}) collective-permute-start(bf16[512,1152]{1,0:T(8,128)(2,1)S(1)} %fusion.15.grad_ref), channel_id=1, source_target_pairs={{0,16},{4,20},{8,24},{12,28},{16,0},{20,4},{24,8},{28,12},{1,17},{... | collective-permute-start | bytes 3538952 | tf_op jit(solution)/shard_map/ppermute | solution.py:101
  41.4 27.0 %collective-permute-start.9 = (bf16[256,1152]{1,0:T(8,128)(2,1)S(1)}, bf16[256,1152]{1,0:T(8,128)(2,1)S(1)}, u32[]{:S(2)}, u32[]{:S(2)}) collective-permute-start(bf16[256,1152]{1,0:T(8,128)(2,1)S(1)} %slice.311), channel_id=1, source_target_pairs={{0,16},{4,20},{8,24},{12,28},{16,0},{20,4},{24,8},{28,12},{1,17},{... | collective-permute-start | bytes 1769480 | tf_op jit(solution)/shard_map/ppermute | solution.py:101
  43.8 25.4 %collective-permute-start.10 = (bf16[256,1152]{1,0:T(8,128)(2,1)S(1)}, bf16[256,1152]{1,0:T(8,128)(2,1)S(1)}, u32[]{:S(2)}, u32[]{:S(2)}) collective-permute-start(bf16[256,1152]{1,0:T(8,128)(2,1)S(1)} %slice.312), channel_id=1, source_target_pairs={{0,8},{4,12},{8,0},{12,4},{16,24},{20,28},{24,16},{28,20},{1,9},{5... | collective-permute-start | bytes 1769480 | tf_op jit(solution)/shard_map/ppermute | solution.py:101
  69.7 27.4 %collective-permute-start.15 = (bf16[512,1024]{1,0:T(8,128)(2,1)S(1)}, bf16[512,1024]{1,0:T(8,128)(2,1)S(1)}, u32[]{:S(2)}, u32[]{:S(2)}) collective-permute-start(bf16[512,1024]{1,0:T(8,128)(2,1)S(1)} %multiply_convert_fusion.normed_ref), channel_id=1, source_target_pairs={{0,16},{4,20},{8,24},{12,28},{16,0},{20,4},{24,8},{28,12},{1,17},{... | collective-permute-start | bytes 3145736 | tf_op jit(solution)/shard_map/ppermute | solution.py:101
  70.9 24.0 %collective-permute-start.14 = (bf16[512,1024]{1,0:T(8,128)(2,1)S(1)}, bf16[512,1024]{1,0:T(8,128)(2,1)}, u32[]{:S(2)}, u32[]{:S(2)}) collective-permute-start(bf16[512,1024]{1,0:T(8,128)(2,1)S(1)} %multiply_convert_fusion.normed_ref), channel_id=1, source_target_pairs={{0,8},{4,12},{8,0},{12,4},{16,24},{20,28},{24,16},{28,20},{1,9},{5... | collective-permute-start | bytes 3145736 | tf_op jit(solution)/shard_map/ppermute | solution.py:101
  71.2 27.0 %collective-permute-start.11 = (bf16[4,1024,128]{2,1,0:T(8,128)(2,1)}, bf16[4,1024,128]{2,1,0:T(8,128)(2,1)}, u32[]{:S(2)}, u32[]{:S(2)}) collective-permute-start(bf16[4,1024,128]{2,1,0:T(8,128)(2,1)} %param.29), channel_id=1, source_target_pairs={{0,4},{4,0},{8,12},{12,8},{16,20},{20,16},{24,28},{28,24},{1,5},{5... | collective-permute-start | bytes 3145736 | tf_op jit(solution)/shard_map/ppermute | solution.py:101
  72.9 27.2 %collective-permute-start.12 = (bf16[4,1024,128]{2,1,0:T(8,128)(2,1)}, bf16[4,1024,128]{2,1,0:T(8,128)(2,1)}, u32[]{:S(2)}, u32[]{:S(2)}) collective-permute-start(bf16[4,1024,128]{2,1,0:T(8,128)(2,1)} %param.30), channel_id=1, source_target_pairs={{0,4},{4,0},{8,12},{12,8},{16,20},{20,16},{24,28},{28,24},{1,5},{5... | collective-permute-start | bytes 3145736 | tf_op jit(solution)/shard_map/ppermute | solution.py:101
  73.0 30.0 %collective-permute-start.13 = (bf16[4,128,1024]{2,1,0:T(8,128)(2,1)}, bf16[4,128,1024]{2,1,0:T(8,128)(2,1)}, u32[]{:S(2)}, u32[]{:S(2)}) collective-permute-start(bf16[4,128,1024]{2,1,0:T(8,128)(2,1)} %param.31), channel_id=1, source_target_pairs={{0,4},{4,0},{8,12},{12,8},{16,20},{20,16},{24,28},{28,24},{1,5},{5... | collective-permute-start | bytes 3145736 | tf_op jit(solution)/shard_map/ppermute | solution.py:101
  96.8 55.3 %collective-permute-start.19 = (bf16[256,1024]{1,0:T(8,128)(2,1)}, bf16[256,1024]{1,0:T(8,128)(2,1)S(1)}, u32[]{:S(2)}, u32[]{:S(2)}) collective-permute-start(bf16[256,1024]{1,0:T(8,128)(2,1)} %slice.314), channel_id=1, source_target_pairs={{0,16},{4,20},{8,24},{12,28},{16,0},{20,4},{24,8},{28,12},{1,17},{... | collective-permute-start | bytes 1572872 | tf_op jit(solution)/shard_map/ppermute | solution.py:101
  97.9 62.7 %collective-permute-start.16 = (bf16[256,1024]{1,0:T(8,128)(2,1)}, bf16[256,1024]{1,0:T(8,128)(2,1)S(1)}, u32[]{:S(2)}, u32[]{:S(2)}) collective-permute-start(bf16[256,1024]{1,0:T(8,128)(2,1)} %slice.313), channel_id=1, source_target_pairs={{0,8},{4,12},{8,0},{12,4},{16,24},{20,28},{24,16},{28,20},{1,9},{5... | collective-permute-start | bytes 1572872 | tf_op jit(solution)/shard_map/ppermute | solution.py:101
  159.5 38.0 %collective-permute-start.20 = (bf16[256,1152]{1,0:T(8,128)(2,1)}, bf16[256,1152]{1,0:T(8,128)(2,1)}, u32[]{:S(2)}, u32[]{:S(2)}) collective-permute-start(bf16[256,1152]{1,0:T(8,128)(2,1)} %get-tuple-element.159), channel_id=1, source_target_pairs={{0,8},{4,12},{8,0},{12,4},{16,24},{20,28},{24,16},{28,20},{1,9},{5... | collective-permute-start | bytes 1769480 | tf_op jit(solution)/shard_map/ppermute | solution.py:101
  165.6 33.6 %collective-permute-start.17 = (bf16[256,1152]{1,0:T(8,128)(2,1)}, bf16[256,1152]{1,0:T(8,128)(2,1)}, u32[]{:S(2)}, u32[]{:S(2)}) collective-permute-start(bf16[256,1152]{1,0:T(8,128)(2,1)} %get-tuple-element.155), channel_id=1, source_target_pairs={{0,16},{4,20},{8,24},{12,28},{16,0},{20,4},{24,8},{28,12},{1,17},{... | collective-permute-start | bytes 1769480 | tf_op jit(solution)/shard_map/ppermute | solution.py:101
  198.9 24.8 %collective-permute-start.21 = (bf16[512,1152]{1,0:T(8,128)(2,1)S(1)}, bf16[512,1152]{1,0:T(8,128)(2,1)S(1)}, u32[]{:S(2)}, u32[]{:S(2)}) collective-permute-start(bf16[512,1152]{1,0:T(8,128)(2,1)S(1)} %fusion.31), channel_id=1, source_target_pairs={{0,16},{4,20},{8,24},{12,28},{16,0},{20,4},{24,8},{28,12},{1,17},{... | collective-permute-start | bytes 3538952 | tf_op jit(solution)/shard_map/ppermute | solution.py:101
  200.5 24.5 %collective-permute-start.18 = (bf16[512,1152]{1,0:T(8,128)(2,1)S(1)}, bf16[512,1152]{1,0:T(8,128)(2,1)S(1)}, u32[]{:S(2)}, u32[]{:S(2)}) collective-permute-start(bf16[512,1152]{1,0:T(8,128)(2,1)S(1)} %fusion.30), channel_id=1, source_target_pairs={{0,8},{4,12},{8,0},{12,4},{16,24},{20,28},{24,16},{28,20},{1,9},{5... | collective-permute-start | bytes 3538952 | tf_op jit(solution)/shard_map/ppermute | solution.py:101
  229.3 23.9 %collective-permute-start.29 = (bf16[128,1152]{1,0:T(8,128)(2,1)S(1)}, bf16[128,1152]{1,0:T(8,128)(2,1)S(1)}, u32[]{:S(2)}, u32[]{:S(2)}) collective-permute-start(bf16[128,1152]{1,0:T(8,128)(2,1)S(1)} %get-tuple-element.226), channel_id=1, source_target_pairs={{0,1},{1,2},{2,3},{3,0},{4,5},{5,6},{6,7},{7,4},{8,9},{9,10},{10,1... | collective-permute-start | bytes 884744 | tf_op jit(solution)/shard_map/ppermute | solution.py:106
  234.1 27.3 %collective-permute-start.24 = (bf16[256,1024]{1,0:T(8,128)(2,1)S(1)}, bf16[256,1024]{1,0:T(8,128)(2,1)S(1)}, u32[]{:S(2)}, u32[]{:S(2)}) collective-permute-start(bf16[256,1024]{1,0:T(8,128)(2,1)S(1)} %copy-done.39), channel_id=1, source_target_pairs={{0,8},{4,12},{8,0},{12,4},{16,24},{20,28},{24,16},{28,20},{1,9},{5... | collective-permute-start | bytes 1572872 | tf_op jit(solution)/shard_map/ppermute | solution.py:101
  234.4 29.5 %collective-permute-start.22 = (bf16[256,1024]{1,0:T(8,128)(2,1)S(1)}, bf16[256,1024]{1,0:T(8,128)(2,1)S(1)}, u32[]{:S(2)}, u32[]{:S(2)}) collective-permute-start(bf16[256,1024]{1,0:T(8,128)(2,1)S(1)} %copy-done.41), channel_id=1, source_target_pairs={{0,16},{4,20},{8,24},{12,28},{16,0},{20,4},{24,8},{28,12},{1,17},{... | collective-permute-start | bytes 1572872 | tf_op jit(solution)/shard_map/ppermute | solution.py:101
  263.9 30.6 %collective-permute-start.36 = (bf16[176,1024]{1,0:T(8,128)(2,1)S(1)}, bf16[176,1024]{1,0:T(8,128)(2,1)S(1)}, u32[]{:S(2)}, u32[]{:S(2)}) collective-permute-start(bf16[176,1024]{1,0:T(8,128)(2,1)S(1)} %pad_maximum_fusion.4), channel_id=1, source_target_pairs={{0,2},{1,3},{2,0},{3,1},{4,6},{5,7},{6,4},{7,5},{8,10},{9,11},{10,... | collective-permute-start | bytes 1081352 | tf_op jit(solution)/shard_map/ppermute | solution.py:106
  267.0 30.5 %collective-permute-start.37 = (bf16[176,1024]{1,0:T(8,128)(2,1)S(1)}, bf16[176,1024]{1,0:T(8,128)(2,1)S(1)}, u32[]{:S(2)}, u32[]{:S(2)}) collective-permute-start(bf16[176,1024]{1,0:T(8,128)(2,1)S(1)} %pad_maximum_fusion.4), channel_id=1, source_target_pairs={{0,3},{1,0},{2,1},{3,2},{4,7},{5,4},{6,5},{7,6},{8,11},{9,8},{10,9... | collective-permute-start | bytes 1081352 | tf_op jit(solution)/shard_map/ppermute | solution.py:106
  268.8 46.1 %collective-permute-start.25 = (bf16[512,1024]{1,0:T(8,128)(2,1)S(1)}, bf16[512,1024]{1,0:T(8,128)(2,1)S(1)}, u32[]{:S(2)}, u32[]{:S(2)}) collective-permute-start(bf16[512,1024]{1,0:T(8,128)(2,1)S(1)} %fusion.33), channel_id=1, source_target_pairs={{0,16},{4,20},{8,24},{12,28},{16,0},{20,4},{24,8},{28,12},{1,17},{... | collective-permute-start | bytes 3145736 | tf_op jit(solution)/shard_map/ppermute | solution.py:101
  271.6 43.4 %collective-permute-start.23 = (bf16[512,1024]{1,0:T(8,128)(2,1)S(1)}, bf16[512,1024]{1,0:T(8,128)(2,1)S(1)}, u32[]{:S(2)}, u32[]{:S(2)}) collective-permute-start(bf16[512,1024]{1,0:T(8,128)(2,1)S(1)} %fusion.32), channel_id=1, source_target_pairs={{0,8},{4,12},{8,0},{12,4},{16,24},{20,28},{24,16},{28,20},{1,9},{5... | collective-permute-start | bytes 3145736 | tf_op jit(solution)/shard_map/ppermute | solution.py:101
  324.3 47.1 %collective-permute-start.47 = (bf16[832,512]{1,0:T(8,128)(2,1)}, bf16[832,512]{1,0:T(8,128)(2,1)}, u32[]{:S(2)}, u32[]{:S(2)}) collective-permute-start(bf16[832,512]{1,0:T(8,128)(2,1)} %constant_dynamic-slice_fusion), channel_id=1, source_target_pairs={{0,4},{4,0},{8,12},{12,8},{16,20},{20,16},{24,28},{28,24},{1,5},{5... | collective-permute-start | bytes 2555912 | tf_op jit(solution)/shard_map/ppermute | solution.py:101
  398.7 26.1 %collective-permute-start.54 = (bf16[832,512]{1,0:T(8,128)(2,1)S(1)}, bf16[832,512]{1,0:T(8,128)(2,1)S(1)}, u32[]{:S(2)}, u32[]{:S(2)}) collective-permute-start(bf16[832,512]{1,0:T(8,128)(2,1)S(1)} %constant_dynamic-update-slice_fusion.1), channel_id=1, source_target_pairs={{0,4},{4,0},{8,12},{12,8},{16,20},{20,16},{24,28},{28,24},{1,5},{5... | collective-permute-start | bytes 2555912 | tf_op jit(solution)/shard_map/ppermute | solution.py:101
  (124 other events, 876.4 us)
where the time goes:
time: 436 us; the launch traced here: 430 us
  waiting for transfers between devices  172 us (39%)
  matrix products  62.9 us (14%)
  starting transfers between devices  60.5 us (14%)
  other arithmetic  46.8 us (11%)
  local copies, waits for them, and re-layouts  43.4 us (10%)
  Pallas kernels  42.1 us (10%)
    ppermute x24, waiting for transfers between devices, z_shift(): lax.ppermute(array, 'tensor', [(i, (i + step) % size) for i in range(size)])  126 us
    ppermute x31, waiting for transfers between devices, swap(): return lax.ppermute(array, 'expert', [(i, i ^ mask) for i in range(size)])  46.2 us
    dot_general x17, matrix products, mm_rows(): lax.dot_general(left, right, (((0,), (0,)), ((), ())), preferred_element_...  43.2 us
    pallas_call x5, Pallas kernels, expert_block(): pl.pallas_call(functools.partial(expert_kernel, experts, top_count, units...  42.1 us
    ppermute x24, starting transfers between devices, z_shift(): lax.ppermute(array, 'tensor', [(i, (i + step) % size) for i in range(size)])  32.6 us
    ppermute x31, starting transfers between devices, swap(): return lax.ppermute(array, 'expert', [(i, i ^ mask) for i in range(size)])  27.9 us
    unnamed x192, local copies, waits for them, and re-layouts  27.8 us
    dot_general x8, matrix products, mm(): return jnp.dot(left, right, preferred_element_type=F32)  9.3 us
  transfers between devices with their start and end apart: 55, of which 24 were waited for; matrix products, arithmetic and copies ran while one was open for 26% of the time, Pallas kernels for 10%

commit v1 on v0

--- a/solution.py
+++ b/solution.py
@@ -155,14 +155,15 @@
             scatter_dimension=0,
             tiled=True,
             axis_index_groups=same_core_groups(),
-        ).astype(F32)
+        ).astype(F32), ()
     own, for_x, for_y, far_x, far_y = blocks
     half = own.shape[0] // 2
     via_x = swap(far_x, 2).astype(F32)
     via_y = swap(far_y, 4).astype(F32)
     for_y = for_y.at[:half].set((for_y[:half].astype(F32) + via_x).astype(BF16))
     for_x = for_x.at[half:].set((for_x[half:].astype(F32) + via_y).astype(BF16))
-    return own.astype(F32) + swap(for_x, 2).astype(F32) + swap(for_y, 4).astype(F32)
+    total = own.astype(F32) + swap(for_x, 2).astype(F32) + swap(for_y, 4).astype(F32)
+    return total, (for_x, for_y)
 
 
 def expert_sum(array):
@@ -363,6 +364,9 @@
     w_halves = [z_shift(piece(w_output, core, half), step) for step in range(1, tensor_count)]
     expert_weights = [expert_gate_weight, expert_up_weight, expert_down_weight]
     if expert_count == 8:
+        w_halves, expert_weights = tied(w_halves, expert_weights)
+    other_weights = [swap(weight, 1) for weight in expert_weights]
+    if expert_count == 8:
         grad_blocks, w_halves = tied(grad_blocks, w_halves)
     w_halves = jnp.stack(w_halves)
     w_others = swap(w_halves, 1)
@@ -391,12 +395,12 @@
     attended, log_total = attend_forward(query_rows, rotated_keys, value_rows)
     attended = attended.reshape(tok_count, heads_query * HEAD_DIMENSION)
 
+    attended, other_weights = tied(attended, other_weights)
     attended_parts = z_received(attended)
 
-    resid_in, attended_parts, expert_weights, w_parts = tied(
-        resid_in, attended_parts, expert_weights, w_parts
-    )
-    other_weights = [swap(weight, 1) for weight in expert_weights]
+    resid_in, attended_parts, other_weights, w_parts = tied(
+        resid_in, attended_parts, other_weights, w_parts
+    )
     attended = attended_parts[0]
 
     def as_columns(weight):
@@ -421,9 +425,9 @@
     if expert_count == 8:
         second_norm, grad_far = tied(second_norm, grad_far)
         grad_blocks = grad_blocks + grad_far
-    normed_blocks = plane_gather(second_norm)
-    done = [
-        expert_block(
+
+    def through_experts(normed, grad):
+        return expert_block(
             local_names,
             normed,
             grad,
@@ -435,11 +439,24 @@
             top_count,
             units,
         )
-        for normed, grad in zip(normed_blocks, grad_blocks)
-    ]
-    plane_rows = plane_scatter([block[1] for block in done])
+
+    if expert_count == 8:
+        half = tok_count // 2
+        from_x, from_y = swap(second_norm, 2), swap(second_norm, 4)
+        own_done = through_experts(second_norm, grad_blocks[0])
+        from_x, from_y, own_done = tied(from_x, from_y, own_done)
+        normed_blocks = [
+            second_norm, from_x, from_y, swap(from_x[:half], 4), swap(from_y[half:], 2)
+        ]
+        done = [own_done]
+    else:
+        normed_blocks = plane_gather(second_norm)
+        done = []
+    for normed, grad in list(zip(normed_blocks, grad_blocks))[len(done) :]:
+        done.append(through_experts(normed, grad))
+    plane_rows, merged = plane_scatter([block[1] for block in done])
     plane_rows, *out_blocks = tied(plane_rows, *[block[0] for block in done])
-    held = tied(*[array for block in done for array in block[2:]])
+    held, merged = tied([array for block in done for array in block[2:]], merged)
     done = [held[3 * i : 3 * i + 3] for i in range(len(done))]
     gate_total = up_total = down_total = 0.0
     for normed, grad, block in zip(normed_blocks, grad_blocks, done):
@@ -448,7 +465,7 @@
         down_total = down_total + mm_rows(block[2], grad[:, :model_width])
 
     row_sum = z_scatter(plane_rows)
-    plane_out = plane_scatter(out_blocks)
+    plane_out, _ = plane_scatter(out_blocks)
     row_sum, gate_total, up_total, down_total = tied(row_sum, gate_total, up_total, down_total)
 
     width = here * units
@@ -524,7 +541,7 @@
         + mm_cols(grad_key_raw, key_projection_weight)
         + mm_cols(grad_value_raw, value_projection_weight)
     )
-    norm1_part = sum(z_received(jnp.sum(grad_first * resid_in * first_scale, axis=0)[None]))
+    norm1_part = jnp.sum(grad_first * resid_in * first_scale, axis=0)[None]
 
     grad_raw = mm_rows(first_norm, grad_raw)
     raw_width = grad_raw.shape[1]
@@ -549,7 +566,7 @@
 
     grad_output = unfolded(1, grad_output.shape[0])
     small = unfolded(1 + folds, experts + 1)
-    grad_norm1 = unfolded(1 + 2 * folds, 1)[0]
+    grad_norm1 = sum(z_received(unfolded(1 + 2 * folds, 1)))[0]
     q_width, k_width = w_query.shape[1], key_projection_weight.shape[1]
 
     mixed, grad_first = tied(mixed, grad_first)

time: 436 us -> 410 us (0.940)
  the two profiles are of different devices: /device:TPU:9 before, /device:TPU:0 now
where the time goes in v1:
time: 410 us; the launch traced here: 404 us
  waiting for transfers between devices  130 us (32%)
  matrix products  72.7 us (18%)
  starting transfers between devices  72 us (18%)
  local copies, waits for them, and re-layouts  44.3 us (11%)
  Pallas kernels  42.8 us (10%)
  other arithmetic  39.9 us (10%)
    ppermute x24, waiting for transfers between devices, z_shift(): lax.ppermute(array, 'tensor', [(i, (i + step) % size) for i in range(size)])  100 us
    dot_general x17, matrix products, mm_rows(): lax.dot_general(left, right, (((0,), (0,)), ((), ())), preferred_element_...  51.6 us
    ppermute x24, starting transfers between devices, z_shift(): lax.ppermute(array, 'tensor', [(i, (i + step) % size) for i in range(size)])  44.9 us
    pallas_call x5, Pallas kernels, expert_block(): pl.pallas_call(functools.partial(expert_kernel, experts, top_count, units...  42.8 us
    ppermute x31, waiting for transfers between devices, swap(): return lax.ppermute(array, 'expert', [(i, i ^ mask) for i in range(size)])  29.3 us
    ppermute x31, starting transfers between devices, swap(): return lax.ppermute(array, 'expert', [(i, i ^ mask) for i in range(size)])  27.1 us
    unnamed x178, local copies, waits for them, and re-layouts  25 us
  transfers between devices with their start and end apart: 55, of which 22 were waited for; matrix products, arithmetic and copies ran while one was open for 31% of the time, Pallas kernels for 11%

profile of v1, /device:TPU:0, one launch (start us, length us, event | category | flops | bytes accessed | tf_op | source)
XLA Modules:
  0.0 403.6 jit_solution(6171727658232204672)
XLA Ops:
  28.7 9.9 %collective-permute-done.9.grad_ref = bf16[512,1152]{1,0:T(8,128)(2,1)S(1)} collective-permute-done((bf16[512,1152]{1,0:T(8,128)(2,1)S(1)}, bf16[512,1152]{1,0:T(8,128)(2,1)S(1)}, u32[]{:S(2)}, u32[]{:S(2)}) %collective-permute-start.9) | collective-permute-done | bytes 1179680 | tf_op jit(solution)/shard_map/ppermute | solution.py:101
  46.0 3.5 fusion.14
  59.0 5.0 %collective-permute-done.6 = bf16[512,256]{0,1:T(8,128)(2,1)S(1)} collective-permute-done((bf16[512,256]{0,1:T(8,128)(2,1)S(1)}, bf16[512,256]{0,1:T(8,128)(2,1)S(1)}, u32[]{:S(2)}, u32[]{:S(2)}) %collective-permute-start.6) | collective-permute-done | bytes 262176 | tf_op jit(solution)/shard_map/ppermute | solution.py:106
  63.9 10.3 %collective-permute-done.7 = bf16[512,256]{0,1:T(8,128)(2,1)S(1)} collective-permute-done((bf16[512,256]{0,1:T(8,128)(2,1)S(1)}, bf16[512,256]{0,1:T(8,128)(2,1)S(1)}, u32[]{:S(2)}, u32[]{:S(2)}) %collective-permute-start.7) | collective-permute-done | bytes 262176 | tf_op jit(solution)/shard_map/ppermute | solution.py:106
  88.7 10.6 %experts.5 = (bf16[512,1024]{1,0:T(8,128)(2,1)S(1)}, bf16[512,1152]{1,0:T(8,128)(2,1)S(1)}, bf16[512,1024]{1,0:T(8,128)(2,1)S(1)}, bf16[512,1024]{1,0:T(8,128)(2,1)S(1)}, bf16[512,1024]{1,0:T(8,128)(2,1)S(1)}) custom-call(s32[8]{0:T(128)S(1)} %pad_add_fusion.names_ref, bf16[512,1024]{1,0:T(8,128)(2,1)S(1)} %multiply_convert_fusion.normed_ref, ...), custom_call_target="tpu_custom_call" | custom-call | flops 6442450944 | bytes 13631488 | tf_op jit(solution)/shard_map/experts/pallas_call | solution.py:273
  106.0 11.2 %experts.8 = (bf16[512,1024]{1,0:T(8,128)(2,1)S(1)}, bf16[512,1152]{1,0:T(8,128)(2,1)S(1)}, bf16[512,1024]{1,0:T(8,128)(2,1)S(1)}, bf16[512,1024]{1,0:T(8,128)(2,1)S(1)}, bf16[512,1024]{1,0:T(8,128)(2,1)S(1)}) custom-call(s32[8]{0:T(128)S(1)} %pad_add_fusion.names_ref, bf16[512,1024]{1,0:T(8,128)(2,1)S(1)} %collective-permute-done.15.normed_ref, ...), custom_call_target="tpu_custom_call" | custom-call | flops 6442450944 | bytes 13631488 | tf_op jit(solution)/shard_map/experts/pallas_call | solution.py:273
  123.2 5.1 %experts.9 = (bf16[256,1024]{1,0:T(8,128)(2,1)S(1)}, bf16[256,1152]{1,0:T(8,128)(2,1)}, bf16[256,1024]{1,0:T(8,128)(2,1)S(1)}, bf16[256,1024]{1,0:T(8,128)(2,1)S(1)}, bf16[256,1024]{1,0:T(8,128)(2,1)S(1)}) custom-call(s32[8]{0:T(128)S(1)} %pad_add_fusion.names_ref, bf16[256,1024]{1,0:T(8,128)(2,1)S(1)} %collective-permute-done.19.normed_ref, ...), custom_call_target="tpu_custom_call" | custom-call | flops 3221225472 | bytes 9961472 | tf_op jit(solution)/shard_map/experts/pallas_call | solution.py:273
  131.5 5.1 %experts.7 = (bf16[256,1024]{1,0:T(8,128)(2,1)S(1)}, bf16[256,1152]{1,0:T(8,128)(2,1)}, bf16[256,1024]{1,0:T(8,128)(2,1)S(1)}, bf16[256,1024]{1,0:T(8,128)(2,1)S(1)}, bf16[256,1024]{1,0:T(8,128)(2,1)S(1)}) custom-call(s32[8]{0:T(128)S(1)} %pad_add_fusion.names_ref, bf16[256,1024]{1,0:T(8,128)(2,1)S(1)} %collective-permute-done.16.normed_ref, ...), custom_call_target="tpu_custom_call" | custom-call | flops 3221225472 | bytes 9961472 | tf_op jit(solution)/shard_map/experts/pallas_call | solution.py:273
  140.6 10.7 %experts.6 = (bf16[512,1024]{1,0:T(8,128)(2,1)S(1)}, bf16[512,1152]{1,0:T(8,128)(2,1)S(1)}, bf16[512,1024]{1,0:T(8,128)(2,1)S(1)}, bf16[512,1024]{1,0:T(8,128)(2,1)S(1)}, bf16[512,1024]{1,0:T(8,128)(2,1)S(1)}) custom-call(s32[8]{0:T(128)S(1)} %pad_add_fusion.names_ref, bf16[512,1024]{1,0:T(8,128)(2,1)S(1)} %collective-permute-done.14.normed_ref, ...), custom_call_target="tpu_custom_call" | custom-call | flops 6442450944 | bytes 13631488 | tf_op jit(solution)/shard_map/experts/pallas_call | solution.py:273
  182.6 6.9 %add_add_fusion = f32[1024,1024]{1,0:T(8,128)} fusion(f32[1024,1024]{1,0:T(8,128)S(1)} %fusion.48, f32[1024,1024]{1,0:T(8,128)S(1)} %fusion.24, f32[1024,1024]{1,0:T(8,128)} %fusion.28, f32[1024,1024]{1,0:T(8,128)} %fusion.26, bf16[256,1024]{1,0:T(8,128)(2,1)S(1)} %copy-done.26, bf16[256,1152]{1,0:T(8,128)(2,1)S(1)} %copy-done.29), kind=kOutput, calls=%fused_computation.9 | convolution fusion | flops 541065216 | bytes 22020096 | tf_op jit(solution)/shard_map/dot_general | solution.py:88
  191.6 8.1 %add_add_fusion.2 = f32[1024,1024]{1,0:T(8,128)} fusion(f32[1024,1024]{1,0:T(8,128)S(1)} %fusion.93, f32[1024,1024]{1,0:T(8,128)} %fusion.92, f32[1024,1024]{1,0:T(8,128)} %fusion.90, f32[1024,1024]{1,0:T(8,128)} %fusion.91, bf16[256,1024]{1,0:T(8,128)(2,1)S(1)} %collective-permute-done.16.normed_ref, bf16[256,1024]{1,0:T(8,128)(2,1)S(1)} %copy-done.24), kind=kOutput, calls=%fused_computation.11 | convolution fusion | flops 541065216 | bytes 22020096 | tf_op jit(solution)/shard_map/dot_general | solution.py:88
  200.2 5.2 %collective-permute-start.31 = (bf16[128,1152]{1,0:T(8,128)(2,1)S(1)}, bf16[128,1152]{1,0:T(8,128)(2,1)S(1)}, u32[]{:S(2)}, u32[]{:S(2)}) collective-permute-start(bf16[128,1152]{1,0:T(8,128)(2,1)S(1)} %get-tuple-element.261), channel_id=1, source_target_pairs={{0,3},{1,0},{2,1},{3,2},{4,7},{5,4},{6,5},{7,6},{8,11},{9,8},{10,9... | collective-permute-start | bytes 884744 | tf_op jit(solution)/shard_map/ppermute | solution.py:106
  207.9 5.7 %add_add_fusion.1 = f32[1024,1024]{1,0:T(8,128)} fusion(f32[1024,1024]{1,0:T(8,128)S(1)} %fusion.97, f32[1024,1024]{1,0:T(8,128)S(1)} %fusion.96, f32[1024,1024]{1,0:T(8,128)S(1)} %copy-done.46, f32[1024,1024]{1,0:T(8,128)} %fusion.95, bf16[256,1024]{1,0:T(8,128)(2,1)S(1)} %collective-permute-done.16.normed_ref, bf16[256,1024]{1,0:T(8,128)(2,1)S(1)} %get-tuple-element.229), kind=kOutput, calls=%fused_computation.10 | convolution fusion | flops 541065216 | bytes 22020096 | tf_op jit(solution)/shard_map/dot_general | solution.py:88
  216.6 13.7 %collective-permute-done.30 = bf16[128,1152]{1,0:T(8,128)(2,1)S(1)} collective-permute-done((bf16[128,1152]{1,0:T(8,128)(2,1)S(1)}, bf16[128,1152]{1,0:T(8,128)(2,1)S(1)}, u32[]{:S(2)}, u32[]{:S(2)}) %collective-permute-start.30) | collective-permute-done | bytes 294944 | tf_op jit(solution)/shard_map/ppermute | solution.py:106
  238.4 3.7 collective-permute-start.37
  250.9 14.8 %collective-permute-done.36 = bf16[176,1024]{1,0:T(8,128)(2,1)S(1)} collective-permute-done((bf16[176,1024]{1,0:T(8,128)(2,1)S(1)}, bf16[176,1024]{1,0:T(8,128)(2,1)S(1)}, u32[]{:S(2)}, u32[]{:S(2)}) %collective-permute-start.36) | collective-permute-done | bytes 360480 | tf_op jit(solution)/shard_map/ppermute | solution.py:106
  283.3 7.0 %collective-permute-start.28 = (bf16[512,256]{1,0:T(8,128)(2,1)}, bf16[512,256]{1,0:T(8,128)(2,1)}, u32[]{:S(2)}, u32[]{:S(2)}) collective-permute-start(bf16[512,256]{1,0:T(8,128)(2,1)} %get-tuple-element.267), channel_id=1, source_target_pairs={{0,3},{1,0},{2,1},{3,2},{4,7},{5,4},{6,5},{7,6},{8,11},{9,8},{10,9... | collective-permute-start | bytes 786440 | tf_op jit(solution)/shard_map/ppermute | solution.py:106
  297.4 18.0 %collective-permute-done.27 = bf16[512,256]{1,0:T(8,128)(2,1)} collective-permute-done((bf16[512,256]{1,0:T(8,128)(2,1)}, bf16[512,256]{1,0:T(8,128)(2,1)}, u32[]{:S(2)}, u32[]{:S(2)}) %collective-permute-start.27) | collective-permute-done | bytes 262176 | tf_op jit(solution)/shard_map/ppermute | solution.py:106
  322.8 4.6 %collective-permute-done.40 = bf16[128,1024]{1,0:T(8,128)(2,1)S(1)} collective-permute-done((bf16[128,1024]{1,0:T(8,128)(2,1)}, bf16[128,1024]{1,0:T(8,128)(2,1)S(1)}, u32[]{:S(2)}, u32[]{:S(2)}) %collective-permute-start.40) | collective-permute-done | bytes 262176 | tf_op jit(solution)/shard_map/ppermute | solution.py:106
  327.4 16.9 %collective-permute-done.39 = bf16[128,1024]{1,0:T(8,128)(2,1)} collective-permute-done((bf16[128,1024]{1,0:T(8,128)(2,1)}, bf16[128,1024]{1,0:T(8,128)(2,1)}, u32[]{:S(2)}, u32[]{:S(2)}) %collective-permute-start.39) | collective-permute-done | bytes 262176 | tf_op jit(solution)/shard_map/ppermute | solution.py:106
  350.8 5.6 %collective-permute-done.47 = bf16[208,512]{1,0:T(8,128)(2,1)S(1)} collective-permute-done((bf16[208,512]{1,0:T(8,128)(2,1)S(1)}, bf16[208,512]{1,0:T(8,128)(2,1)S(1)}, u32[]{:S(2)}, u32[]{:S(2)}) %collective-permute-start.47) | collective-permute-done | bytes 213024 | tf_op jit(solution)/shard_map/ppermute | solution.py:101
  367.2 3.4 collective-permute-done.49
  375.0 12.3 %collective-permute-done.42 = bf16[128,1024]{1,0:T(8,128)(2,1)S(1)} collective-permute-done((bf16[128,1024]{1,0:T(8,128)(2,1)S(1)}, bf16[128,1024]{1,0:T(8,128)(2,1)S(1)}, u32[]{:S(2)}, u32[]{:S(2)}) %collective-permute-start.42) | collective-permute-done | bytes 262176 | tf_op jit(solution)/shard_map/ppermute | solution.py:106
  390.0 7.2 %collective-permute-start.54 = (f32[1,1024]{1,0:T(1,128)S(1)}, f32[1,1024]{1,0:T(1,128)S(1)}, u32[]{:S(2)}, u32[]{:S(2)}) collective-permute-start(f32[1,1024]{1,0:T(1,128)S(1)} %pad_maximum_fusion.12), channel_id=1, source_target_pairs={{0,3},{1,0},{2,1},{3,2},{4,7},{5,4},{6,5},{7,6},{8,11},{9,8},{10,9... | collective-permute-start | bytes 12296 | tf_op jit(solution)/shard_map/ppermute | solution.py:106
  (407 shorter events, 196.6 us)
Async XLA Ops:
  2.4 25.6 %collective-permute-start = (bf16[128,1024]{1,0:T(8,128)(2,1)}, bf16[128,1024]{1,0:T(8,128)(2,1)S(1)}, u32[]{:S(2)}, u32[]{:S(2)}) collective-permute-start(bf16[128,1024]{1,0:T(8,128)(2,1)} %constant_dynamic-slice_fusion.2), channel_id=1, source_target_pairs={{0,1},{1,2},{2,3},{3,0},{4,5},{5,6},{6,7},{7,4},{8,9},{9,10},{10,1... | collective-permute-start | bytes 786440 | tf_op jit(solution)/shard_map/ppermute | solution.py:106
  11.7 26.9 %collective-permute-start.9 = (bf16[512,1152]{1,0:T(8,128)(2,1)S(1)}, bf16[512,1152]{1,0:T(8,128)(2,1)S(1)}, u32[]{:S(2)}, u32[]{:S(2)}) collective-permute-start(bf16[512,1152]{1,0:T(8,128)(2,1)S(1)} %fusion.15.grad_ref), channel_id=1, source_target_pairs={{0,8},{4,12},{8,0},{12,4},{16,24},{20,28},{24,16},{28,20},{1,9},{5... | collective-permute-start | bytes 3538952 | tf_op jit(solution)/shard_map/ppermute | solution.py:101
  13.3 26.7 %collective-permute-start.10 = (bf16[512,1152]{1,0:T(8,128)(2,1)S(1)}, bf16[512,1152]{1,0:T(8,128)(2,1)}, u32[]{:S(2)}, u32[]{:S(2)}) collective-permute-start(bf16[512,1152]{1,0:T(8,128)(2,1)S(1)} %fusion.15.grad_ref), channel_id=1, source_target_pairs={{0,16},{4,20},{8,24},{12,28},{16,0},{20,4},{24,8},{28,12},{1,17},{... | collective-permute-start | bytes 3538952 | tf_op jit(solution)/shard_map/ppermute | solution.py:101
  28.0 24.2 %collective-permute-start.3 = (bf16[4,1024,128]{2,1,0:T(8,128)(2,1)}, bf16[4,1024,128]{2,1,0:T(8,128)(2,1)}, u32[]{:S(2)}, u32[]{:S(2)}) collective-permute-start(bf16[4,1024,128]{2,1,0:T(8,128)(2,1)} %param.29), channel_id=1, source_target_pairs={{0,4},{4,0},{8,12},{12,8},{16,20},{20,16},{24,28},{28,24},{1,5},{5... | collective-permute-start | bytes 3145736 | tf_op jit(solution)/shard_map/ppermute | solution.py:101
  28.1 24.8 %collective-permute-start.4 = (bf16[4,1024,128]{2,1,0:T(8,128)(2,1)}, bf16[4,1024,128]{2,1,0:T(8,128)(2,1)}, u32[]{:S(2)}, u32[]{:S(2)}) collective-permute-start(bf16[4,1024,128]{2,1,0:T(8,128)(2,1)} %param.30), channel_id=1, source_target_pairs={{0,4},{4,0},{8,12},{12,8},{16,20},{20,16},{24,28},{28,24},{1,5},{5... | collective-permute-start | bytes 3145736 | tf_op jit(solution)/shard_map/ppermute | solution.py:101
  28.6 24.3 %collective-permute-start.5 = (bf16[4,128,1024]{2,1,0:T(8,128)(2,1)}, bf16[4,128,1024]{2,1,0:T(8,128)(2,1)}, u32[]{:S(2)}, u32[]{:S(2)}) collective-permute-start(bf16[4,128,1024]{2,1,0:T(8,128)(2,1)} %param.31), channel_id=1, source_target_pairs={{0,4},{4,0},{8,12},{12,8},{16,20},{20,16},{24,28},{28,24},{1,5},{5... | collective-permute-start | bytes 3145736 | tf_op jit(solution)/shard_map/ppermute | solution.py:101
  49.6 28.5 %collective-permute-start.12 = (bf16[256,1152]{1,0:T(8,128)(2,1)S(1)}, bf16[256,1152]{1,0:T(8,128)(2,1)S(1)}, u32[]{:S(2)}, u32[]{:S(2)}) collective-permute-start(bf16[256,1152]{1,0:T(8,128)(2,1)S(1)} %slice.311), channel_id=1, source_target_pairs={{0,16},{4,20},{8,24},{12,28},{16,0},{20,4},{24,8},{28,12},{1,17},{... | collective-permute-start | bytes 1769480 | tf_op jit(solution)/shard_map/ppermute | solution.py:101
  52.3 25.8 %collective-permute-start.13 = (bf16[256,1152]{1,0:T(8,128)(2,1)S(1)}, bf16[256,1152]{1,0:T(8,128)(2,1)S(1)}, u32[]{:S(2)}, u32[]{:S(2)}) collective-permute-start(bf16[256,1152]{1,0:T(8,128)(2,1)S(1)} %slice.312), channel_id=1, source_target_pairs={{0,8},{4,12},{8,0},{12,4},{16,24},{20,28},{24,16},{28,20},{1,9},{5... | collective-permute-start | bytes 1769480 | tf_op jit(solution)/shard_map/ppermute | solution.py:101
  78.9 23.9 %collective-permute-start.14 = (bf16[512,1024]{1,0:T(8,128)(2,1)S(1)}, bf16[512,1024]{1,0:T(8,128)(2,1)S(1)}, u32[]{:S(2)}, u32[]{:S(2)}) collective-permute-start(bf16[512,1024]{1,0:T(8,128)(2,1)S(1)} %multiply_convert_fusion.normed_ref), channel_id=1, source_target_pairs={{0,8},{4,12},{8,0},{12,4},{16,24},{20,28},{24,16},{28,20},{1,9},{5... | collective-permute-start | bytes 3145736 | tf_op jit(solution)/shard_map/ppermute | solution.py:101
  80.4 23.6 %collective-permute-start.15 = (bf16[512,1024]{1,0:T(8,128)(2,1)S(1)}, bf16[512,1024]{1,0:T(8,128)(2,1)S(1)}, u32[]{:S(2)}, u32[]{:S(2)}) collective-permute-start(bf16[512,1024]{1,0:T(8,128)(2,1)S(1)} %multiply_convert_fusion.normed_ref), channel_id=1, source_target_pairs={{0,16},{4,20},{8,24},{12,28},{16,0},{20,4},{24,8},{28,12},{1,17},{... | collective-permute-start | bytes 3145736 | tf_op jit(solution)/shard_map/ppermute | solution.py:101
  105.5 26.1 %collective-permute-start.16 = (bf16[256,1024]{1,0:T(8,128)(2,1)}, bf16[256,1024]{1,0:T(8,128)(2,1)S(1)}, u32[]{:S(2)}, u32[]{:S(2)}) collective-permute-start(bf16[256,1024]{1,0:T(8,128)(2,1)} %slice.259), channel_id=1, source_target_pairs={{0,8},{4,12},{8,0},{12,4},{16,24},{20,28},{24,16},{28,20},{1,9},{5... | collective-permute-start | bytes 1572872 | tf_op jit(solution)/shard_map/ppermute | solution.py:101
  152.7 46.9 %collective-permute-start.21 = (bf16[512,1152]{1,0:T(8,128)(2,1)S(1)}, bf16[512,1152]{1,0:T(8,128)(2,1)S(1)}, u32[]{:S(2)}, u32[]{:S(2)}) collective-permute-start(bf16[512,1152]{1,0:T(8,128)(2,1)S(1)} %fusion.31), channel_id=1, source_target_pairs={{0,16},{4,20},{8,24},{12,28},{16,0},{20,4},{24,8},{28,12},{1,17},{... | collective-permute-start | bytes 3538952 | tf_op jit(solution)/shard_map/ppermute | solution.py:101
  153.6 46.1 %collective-permute-start.18 = (bf16[512,1152]{1,0:T(8,128)(2,1)S(1)}, bf16[512,1152]{1,0:T(8,128)(2,1)S(1)}, u32[]{:S(2)}, u32[]{:S(2)}) collective-permute-start(bf16[512,1152]{1,0:T(8,128)(2,1)S(1)} %fusion.30), channel_id=1, source_target_pairs={{0,8},{4,12},{8,0},{12,4},{16,24},{20,28},{24,16},{28,20},{1,9},{5... | collective-permute-start | bytes 3538952 | tf_op jit(solution)/shard_map/ppermute | solution.py:101
  205.4 24.9 %collective-permute-start.30 = (bf16[128,1152]{1,0:T(8,128)(2,1)S(1)}, bf16[128,1152]{1,0:T(8,128)(2,1)S(1)}, u32[]{:S(2)}, u32[]{:S(2)}) collective-permute-start(bf16[128,1152]{1,0:T(8,128)(2,1)S(1)} %get-tuple-element.262), channel_id=1, source_target_pairs={{0,2},{1,3},{2,0},{3,1},{4,6},{5,7},{6,4},{7,5},{8,10},{9,11},{10,... | collective-permute-start | bytes 884744 | tf_op jit(solution)/shard_map/ppermute | solution.py:106
  213.6 24.1 %collective-permute-start.24 = (bf16[256,1024]{1,0:T(8,128)(2,1)S(1)}, bf16[256,1024]{1,0:T(8,128)(2,1)S(1)}, u32[]{:S(2)}, u32[]{:S(2)}) collective-permute-start(bf16[256,1024]{1,0:T(8,128)(2,1)S(1)} %copy-done.39), channel_id=1, source_target_pairs={{0,8},{4,12},{8,0},{12,4},{16,24},{20,28},{24,16},{28,20},{1,9},{5... | collective-permute-start | bytes 1572872 | tf_op jit(solution)/shard_map/ppermute | solution.py:101
  238.0 27.7 %collective-permute-start.36 = (bf16[176,1024]{1,0:T(8,128)(2,1)S(1)}, bf16[176,1024]{1,0:T(8,128)(2,1)S(1)}, u32[]{:S(2)}, u32[]{:S(2)}) collective-permute-start(bf16[176,1024]{1,0:T(8,128)(2,1)S(1)} %pad_maximum_fusion.4), channel_id=1, source_target_pairs={{0,2},{1,3},{2,0},{3,1},{4,6},{5,7},{6,4},{7,5},{8,10},{9,11},{10,... | collective-permute-start | bytes 1081352 | tf_op jit(solution)/shard_map/ppermute | solution.py:106
  238.4 27.3 %collective-permute-start.37 = (bf16[176,1024]{1,0:T(8,128)(2,1)S(1)}, bf16[176,1024]{1,0:T(8,128)(2,1)S(1)}, u32[]{:S(2)}, u32[]{:S(2)}) collective-permute-start(bf16[176,1024]{1,0:T(8,128)(2,1)S(1)} %pad_maximum_fusion.4), channel_id=1, source_target_pairs={{0,3},{1,0},{2,1},{3,2},{4,7},{5,4},{6,5},{7,6},{8,11},{9,8},{10,9... | collective-permute-start | bytes 1081352 | tf_op jit(solution)/shard_map/ppermute | solution.py:106
  243.8 35.6 %collective-permute-start.25 = (bf16[512,1024]{1,0:T(8,128)(2,1)S(1)}, bf16[512,1024]{1,0:T(8,128)(2,1)S(1)}, u32[]{:S(2)}, u32[]{:S(2)}) collective-permute-start(bf16[512,1024]{1,0:T(8,128)(2,1)S(1)} %fusion.33), channel_id=1, source_target_pairs={{0,16},{4,20},{8,24},{12,28},{16,0},{20,4},{24,8},{28,12},{1,17},{... | collective-permute-start | bytes 3145736 | tf_op jit(solution)/shard_map/ppermute | solution.py:101
  246.9 32.5 %collective-permute-start.23 = (bf16[512,1024]{1,0:T(8,128)(2,1)S(1)}, bf16[512,1024]{1,0:T(8,128)(2,1)S(1)}, u32[]{:S(2)}, u32[]{:S(2)}) collective-permute-start(bf16[512,1024]{1,0:T(8,128)(2,1)S(1)} %fusion.32), channel_id=1, source_target_pairs={{0,8},{4,12},{8,0},{12,4},{16,24},{20,28},{24,16},{28,20},{1,9},{5... | collective-permute-start | bytes 3145736 | tf_op jit(solution)/shard_map/ppermute | solution.py:101
  290.3 25.1 %collective-permute-start.27 = (bf16[512,256]{1,0:T(8,128)(2,1)}, bf16[512,256]{1,0:T(8,128)(2,1)}, u32[]{:S(2)}, u32[]{:S(2)}) collective-permute-start(bf16[512,256]{1,0:T(8,128)(2,1)} %get-tuple-element.268), channel_id=1, source_target_pairs={{0,2},{1,3},{2,0},{3,1},{4,6},{5,7},{6,4},{7,5},{8,10},{9,11},{10,... | collective-permute-start | bytes 786440 | tf_op jit(solution)/shard_map/ppermute | solution.py:106
  292.4 22.9 %collective-permute-start.26 = (bf16[512,256]{1,0:T(8,128)(2,1)S(1)}, bf16[512,256]{1,0:T(8,128)(2,1)}, u32[]{:S(2)}, u32[]{:S(2)}) collective-permute-start(bf16[512,256]{1,0:T(8,128)(2,1)S(1)} %get-tuple-element.266), channel_id=1, source_target_pairs={{0,1},{1,2},{2,3},{3,0},{4,5},{5,6},{6,7},{7,4},{8,9},{9,10},{10,1... | collective-permute-start | bytes 786440 | tf_op jit(solution)/shard_map/ppermute | solution.py:106
  294.6 51.1 %collective-permute-start.44 = (bf16[832,512]{1,0:T(8,128)(2,1)}, bf16[832,512]{1,0:T(8,128)(2,1)}, u32[]{:S(2)}, u32[]{:S(2)}) collective-permute-start(bf16[832,512]{1,0:T(8,128)(2,1)} %constant_dynamic-slice_fusion), channel_id=1, source_target_pairs={{0,4},{4,0},{8,12},{12,8},{16,20},{20,16},{24,28},{28,24},{1,5},{5... | collective-permute-start | bytes 2555912 | tf_op jit(solution)/shard_map/ppermute | solution.py:101
  319.9 24.3 %collective-permute-start.39 = (bf16[128,1024]{1,0:T(8,128)(2,1)}, bf16[128,1024]{1,0:T(8,128)(2,1)}, u32[]{:S(2)}, u32[]{:S(2)}) collective-permute-start(bf16[128,1024]{1,0:T(8,128)(2,1)} %get-tuple-element.265), channel_id=1, source_target_pairs={{0,2},{1,3},{2,0},{3,1},{4,6},{5,7},{6,4},{7,5},{8,10},{9,11},{10,... | collective-permute-start | bytes 786440 | tf_op jit(solution)/shard_map/ppermute | solution.py:106
  320.7 23.6 %collective-permute-start.38 = (bf16[128,1024]{1,0:T(8,128)(2,1)}, bf16[128,1024]{1,0:T(8,128)(2,1)}, u32[]{:S(2)}, u32[]{:S(2)}) collective-permute-start(bf16[128,1024]{1,0:T(8,128)(2,1)} %get-tuple-element.263), channel_id=1, source_target_pairs={{0,1},{1,2},{2,3},{3,0},{4,5},{5,6},{6,7},{7,4},{8,9},{9,10},{10,1... | collective-permute-start | bytes 786440 | tf_op jit(solution)/shard_map/ppermute | solution.py:106
  (117 other events, 826.3 us)
